TPU v7x, 256 devices: a whole 4x4x8 slice. The times are simulated.
256 devices in a mesh: slab: 32 (over x, z), col: 4 (over y), pb: 2 (over core).
Axes of the slice: x: 4, y: 4, z: 8, core: 2. Of those that a mesh axis runs over, the one named last changes fastest.
Arguments:
- queries_raw: float32 [1024, 768], P(('slab', 'col', 'pb')), may hold values from -1.5 to 1.5
- projection: float32 [768, 768], replicated, may hold values from -0.21875 to 0.21875
- passages: bfloat16 [524288, 768], P(('slab', 'col')), may hold values from -17 to 17
- positives: int32 [1024, 4], P(('slab', 'col', 'pb')), may hold values from 0 to 524287
Outputs:
- loss: float32 [1024], P(('slab', 'col', 'pb'))
- grad_raw: float32 [1024, 768], P(('slab', 'col', 'pb'))
- grad_projection: float32 [768, 768], replicated
All inputs are finite; a program needn't handle non-finite values.
Results may differ from a plain program's by a relative error of at most 0.0053.
Values may be sent and summed in bfloat16 or wider, within the bound.
No kernel may reach another device: no remote copies, remote signals or barrier semaphores. Data moves between devices by JAX's collectives and lax.ppermute only.
A program may use at most 128 MiB of HBM per device.

v0:
```python
import jax
import jax.numpy as jnp
from jax import lax
from jax.sharding import Mesh, PartitionSpec as P

POS = 4
ALL = ("x", "z", "y", "c")
XY = ("x", "y")


def exchange(v, axes):
    return lax.all_to_all(v, axes, 0, 0, tiled=False)


def spread(v, axes):
    n = lax.axis_size(axes)
    return exchange(jnp.broadcast_to(v[None], (n,) + v.shape), axes)


def total(v):
    v = jnp.sum(spread(v, XY), axis=0)
    return jnp.sum(spread(v, "z"), axis=0)


def shards(queries_raw, projection, passages, positives):
    hp = lax.Precision.HIGHEST
    rows, dim = passages.shape
    own = queries_raw.shape[0]
    nz, nxy = (lax.axis_size("z"), lax.axis_size(XY))
    plane = nz * own
    queries = nxy * plane
    scale = 1.0 / (4.0 * rows * nz * nxy)
    bf16 = jnp.bfloat16
    raw_all = lax.all_gather(queries_raw.astype(bf16), ALL, axis=0, tiled=True)
    projected = jnp.dot(queries_raw, projection, precision=hp, preferred_element_type=jnp.float32)
    ids = jnp.concatenate([positives >> 14, positives >> 7 & 127, positives & 127], axis=1)
    ids = jnp.pad(ids, ((0, 0), (0, 128 - 3 * POS)))
    packet = jnp.concatenate([projected.astype(bf16), ids.astype(bf16)], axis=1)
    packet = spread(packet, "z").reshape(plane, dim + 128)
    packet = spread(packet, XY).reshape(queries, dim + 128)
    all_emb = packet[:, :dim]
    ids = packet[:, dim : dim + 3 * POS].astype(jnp.float32).astype(jnp.int32)
    all_pos = (ids[:, :POS] << 14) + (ids[:, POS : 2 * POS] << 7) + ids[:, 2 * POS :]
    shard = (lax.axis_index("x") * nz + lax.axis_index("z")) * lax.axis_size("y") + lax.axis_index(
        "y"
    )
    local_pos = all_pos - shard * rows
    scores = lax.dot_general(
        all_emb, passages, (((1,), (1,)), ((), ())), preferred_element_type=jnp.float32
    )
    columns = jnp.arange(rows, dtype=jnp.int32)[None, :]
    owned = [local_pos[:, slot : slot + 1] == columns for slot in range(POS)]
    partial_pos = jnp.stack(
        [jnp.sum(jnp.where(owned[slot], scores, 0.0), axis=1) for slot in range(POS)], axis=0
    )
    pos_scores = total(partial_pos).T
    loss_part = jnp.zeros((queries,), jnp.float32)
    slope_sum = jnp.zeros_like(scores)
    parts = []
    for slot in range(POS):
        sig = jax.nn.sigmoid(scores - pos_scores[:, slot : slot + 1])
        loss_part = loss_part + jnp.sum(sig, axis=1)
        slope = sig * (1.0 - sig)
        slope_sum = slope_sum + slope
        parts.append(-jnp.sum(slope, axis=1))
    sums = total(jnp.stack(parts + [loss_part], axis=0) * scale)
    pos_grad = sums[:POS].T
    grad = slope_sum * scale
    for slot in range(POS):
        grad = grad + jnp.where(owned[slot], pos_grad[:, slot : slot + 1], 0.0)
    part = jnp.dot(grad.astype(bf16), passages, preferred_element_type=jnp.float32)
    part = exchange(part.astype(bf16).reshape(nxy, plane, dim), XY)
    part = jnp.sum(part.astype(jnp.float32), axis=0).astype(bf16)
    summed = jnp.sum(spread(part, "z").astype(jnp.float32), axis=0)
    home = lax.axis_index("z") * own
    query_grad = lax.dynamic_slice_in_dim(summed, home, own, 0)
    grad_raw = jnp.dot(query_grad, projection.T, precision=hp, preferred_element_type=jnp.float32)
    first = lax.axis_index(XY) * plane + home
    loss = lax.dynamic_slice_in_dim(sums[POS], first, own, 0)
    mine = spread(summed.astype(bf16), XY).reshape(queries, dim)
    other = lax.ppermute(mine, "c", [(0, 1), (1, 0)])
    even = lax.axis_index("c") == 0
    grads = jnp.concatenate([jnp.where(even, mine, other), jnp.where(even, other, mine)], axis=0)
    sizes = [lax.axis_size(a) for a in ALL]
    raw = raw_all.reshape(*sizes, own, dim).transpose(3, 0, 2, 1, 4, 5).reshape(2 * queries, dim)
    grad_projection = lax.dot_general(
        raw, grads, (((0,), (0,)), ((), ())), preferred_element_type=jnp.float32
    )
    return (loss, grad_raw, grad_projection)


def solution(mesh):
    axes = Mesh(mesh.devices.reshape(4, 8, 4, 2), ALL)
    in_specs = (P(ALL, None), P(), P(("x", "z", "y"), None), P(ALL, None))
    out_specs = (P(ALL), P(ALL, None), P())
    return jax.shard_map(shards, mesh=axes, in_specs=in_specs, out_specs=out_specs, check_vma=False)
```

profile of v0, /device:TPU:1, one launch (start us, length us, event | category | flops | bytes accessed | tf_op | source)
XLA Modules:
  0.0 247.1 jit_solution(9730011516197225526)
XLA Ops:
  7.2 0.0 copy-start
  7.2 0.8 shift-right-arithmetic_convert_fusion
  8.0 0.8 copy-done
  8.9 1.9 convolution_convert_fusion
  10.8 0.1 fusion.19
  10.9 16.1 %all_to_all.45 = bf16[8,4,896]{2,1,0:T(4,128)(2,1)S(1)} all-to-all(bf16[8,4,896]{2,1,0:T(4,128)(2,1)S(1)} %broadcast_in_dim.93), channel_id=1, replica_groups=mesh['x'=4,'z'=8,'y'=4,'c'=2] {'z'}, dimensions={0} | all-to-all | bytes 114688 | tf_op jit(solution)/shard_map/all_to_all | solution.py:12
  27.0 1.0 broadcast_in_dim.95
  28.0 6.8 %all-to-all-start.1 = ((bf16[16,32,896]{2,1,0:T(8,128)(2,1)}), bf16[16,32,896]{2,1,0:T(8,128)(2,1)S(1)}, u32[]{:S(2)}, u32[]{:S(2)}) async-start(bf16[16,32,896]{2,1,0:T(8,128)(2,1)} %broadcast_in_dim.95), calls=%async_computation.1 | async-start | bytes 1835008 | tf_op jit(solution)/shard_map/all_to_all | solution.py:12
  34.7 13.4 %all-to-all-done.1 = bf16[16,32,896]{2,1,0:T(8,128)(2,1)S(1)} async-done(((bf16[16,32,896]{2,1,0:T(8,128)(2,1)}), bf16[16,32,896]{2,1,0:T(8,128)(2,1)S(1)}, u32[]{:S(2)}, u32[]{:S(2)}) %all-to-all-start.1) | async-done | bytes 917536 | tf_op jit(solution)/shard_map/all_to_all | solution.py:12
  48.1 0.2 fusion.11
  48.3 0.6 slice_reduce_fusion.3
  48.9 11.5 %select_reduce_fusion.3 = (f32[512]{0:T(512)S(1)}, f32[512]{0:T(512)S(1)}, f32[512]{0:T(512)S(1)}, f32[512]{0:T(512)S(1)}, f32[512,4096]{1,0:T(8,128)}) fusion(s32[512]{0:T(512)S(1)} %get-tuple-element.33, s32[512]{0:T(512)S(1)} %get-tuple-element.34, s32[512]{0:T(512)S(1)} %get-tuple-element.35, s32[512]{0:T(512)S(1)} %get-tuple-element.36, ...), kind=kOutput, calls=%fused_computation.15 | convolution fusion | flops 3246389248 | bytes 15482880 | tf_op jit(solution)/shard_map/dot_general | solution.py:48
  60.4 11.2 %all_to_all.46 = f32[16,4,512]{2,1,0:T(4,128)S(1)} all-to-all(f32[16,4,512]{2,1,0:T(4,128)S(1)} %broadcast_in_dim.97), channel_id=1, replica_groups=mesh['x'=4,'z'=8,'y'=4,'c'=2] {'x','y'}, dimensions={0} | all-to-all | bytes 262144 | tf_op jit(solution)/shard_map/all_to_all | solution.py:12
  71.6 9.6 %all_to_all.47 = f32[8,4,512]{2,1,0:T(4,128)S(1)} all-to-all(f32[8,4,512]{2,1,0:T(4,128)S(1)} %broadcast_in_dim.98), channel_id=1, replica_groups=mesh['x'=4,'z'=8,'y'=4,'c'=2] {'z'}, dimensions={0} | all-to-all | bytes 131072 | tf_op jit(solution)/shard_map/all_to_all | solution.py:12
  81.3 0.0 copy-start.1
  81.3 17.0 %fusion.28 = (f32[512]{0:T(512)S(1)}, f32[512]{0:T(512)S(1)}, f32[512,4096]{1,0:T(8,128)}, f32[512]{0:T(512)S(1)}, f32[512]{0:T(512)S(1)}, /*index=5*/f32[512,40...) fusion(f32[512,4096]{1,0:T(8,128)} %get-tuple-element.63, ...), kind=kLoop, calls=%fused_computation.70 | loop fusion | flops 67104768 | bytes 41967616 | tf_op jit(solution)/shard_map/reduce_sum | solution.py:62
  98.5 10.7 %all_to_all.48 = f32[16,5,512]{2,1,0:T(8,128)S(1)} all-to-all(f32[16,5,512]{2,1,0:T(8,128)S(1)} %broadcast_in_dim.99), channel_id=1, replica_groups=mesh['x'=4,'z'=8,'y'=4,'c'=2] {'x','y'}, dimensions={0} | all-to-all | bytes 327680 | tf_op jit(solution)/shard_map/all_to_all | solution.py:12
  109.2 0.7 broadcast_in_dim.100
  109.9 3.4 %all-to-all-start.5 = ((f32[8,5,512]{2,1,0:T(8,128)}), f32[8,5,512]{2,1,0:T(8,128)S(1)}, u32[]{:S(2)}, u32[]{:S(2)}) async-start(f32[8,5,512]{2,1,0:T(8,128)} %broadcast_in_dim.100), calls=%async_computation.5 | async-start | bytes 262144 | tf_op jit(solution)/shard_map/all_to_all | solution.py:12
  113.2 0.2 all-gather.3.cloned.1.call-start
  113.5 0.0 copy-done.1
  113.5 0.6 convert_bitcast_fusion
  114.1 0.0 all-gather.3.cloned.1.call-update
  114.1 7.0 %all-to-all-done.5 = f32[8,5,512]{2,1,0:T(8,128)S(1)} async-done(((f32[8,5,512]{2,1,0:T(8,128)}), f32[8,5,512]{2,1,0:T(8,128)S(1)}, u32[]{:S(2)}, u32[]{:S(2)}) %all-to-all-start.5) | async-done | bytes 81952 | tf_op jit(solution)/shard_map/all_to_all | solution.py:12
  121.1 20.3 %fusion.8 = bf16[512,768]{1,0:T(8,128)(2,1)S(1)} fusion(bf16[4096,768]{1,0:T(8,128)(2,1)} %param.6, f32[512,4096]{1,0:T(8,128)} %get-tuple-element.43, f32[512,4096]{1,0:T(8,128)} %get-tuple-element.49, f32[512,4096]{1,0:T(8,128)} %get-tuple-element.46, f32[512,4096]{1,0:T(8,128)} %get-tuple-element.37, f32[512]{0:T(512)S(1)} %bitcast.58, ...), kind=kOutput, calls=%fused_computation.27 | convolution fusion | flops 3274047488 | bytes 40648704 | tf_op jit(solution)/shard_map/dot_general | solution.py:71
  141.4 13.4 %all_to_all.49 = bf16[16,32,768]{2,1,0:T(8,128)(2,1)S(1)} all-to-all(bf16[16,32,768]{2,1,0:T(8,128)(2,1)S(1)} %bitcast.46), channel_id=1, replica_groups=mesh['x'=4,'z'=8,'y'=4,'c'=2] {'x','y'}, dimensions={0} | all-to-all | bytes 1572864 | tf_op jit(solution)/shard_map/all_to_all | solution.py:12
  154.8 0.1 reduce_sum.181
  154.9 13.1 %all_to_all.50 = bf16[8,32,768]{2,1,0:T(8,128)(2,1)S(1)} all-to-all(bf16[8,32,768]{2,1,0:T(8,128)(2,1)S(1)} %broadcast_in_dim.109), channel_id=1, replica_groups=mesh['x'=4,'z'=8,'y'=4,'c'=2] {'z'}, dimensions={0} | all-to-all | bytes 786432 | tf_op jit(solution)/shard_map/all_to_all | solution.py:12
  168.0 0.1 convert_reduce_fusion
  168.1 0.1 broadcast_in_dim.110
  168.2 13.4 %all_to_all.51 = bf16[16,32,768]{2,1,0:T(8,128)(2,1)S(1)} all-to-all(bf16[16,32,768]{2,1,0:T(8,128)(2,1)S(1)} %broadcast_in_dim.110), channel_id=1, replica_groups=mesh['x'=4,'z'=8,'y'=4,'c'=2] {'x','y'}, dimensions={0} | all-to-all | bytes 1572864 | tf_op jit(solution)/shard_map/all_to_all | solution.py:12
  181.6 10.9 %collective-permute-start = (bf16[512,768]{1,0:T(8,128)(2,1)S(1)}, bf16[512,768]{1,0:T(8,128)(2,1)}, u32[]{:S(2)}, u32[]{:S(2)}) collective-permute-start(bf16[512,768]{1,0:T(8,128)(2,1)S(1)} %bitcast.42), channel_id=1, source_target_pairs={{0,1},{1,0},{2,3},{3,2},{4,5},{5,4},{6,7},{7,6},{8,9},{9,8},{10,11... | collective-permute-start | bytes 2359304 | tf_op jit(solution)/shard_map/ppermute | solution.py:81
  192.5 0.6 dynamic-slice_bitcast_fusion
  193.0 2.6 %fusion.13 = f32[4,768]{1,0:T(4,128)} fusion(f32[768,768]{1,0:T(8,128)S(1)} %copy-done, f32[32,768]{1,0:T(8,128)S(1)} %convert_reduce_fusion, s32[]{:T(128)S(6)} %select_n.53), kind=kOutput, calls=%fused_computation.44 | convolution fusion | flops 28311552 | bytes 2383876 | tf_op jit(solution)/shard_map/dot_general | solution.py:77
  195.7 28.9 %all-gather.3.cloned.1.call-done = bf16[256,4,768]{2,1,0:T(4,128)(2,1)} async-done(((bf16[1,4,768]{2,1,0:T(4,128)(2,1)}), bf16[256,4,768]{2,1,0:T(4,128)(2,1)}) %all-gather.3.cloned.1.call-update) | async-done | bytes 1572880 | tf_op jit(solution)/shard_map/all_gather | solution.py:34
  224.6 3.4 %copy.31 = bf16[4,8,4,2,4,768]{5,4,1,2,0,3:T(4,128)(2,1)} copy(bf16[4,8,4,2,4,768]{5,4,3,2,1,0:T(4,128)(2,1)} %bitcast.43) | data formatting | bytes 3145728 | tf_op jit(solution)/shard_map/reshape | solution.py:85
  228.0 3.7 %reshape.137 = bf16[1024,768]{1,0:T(8,128)(2,1)} reshape(bf16[2,4,4,8,4,768]{5,4,3,2,1,0:T(4,128)(2,1)} %bitcast.41) | data formatting | bytes 3145728 | tf_op jit(solution)/shard_map/reshape | solution.py:85
  231.7 0.0 collective-permute-done
  231.7 1.2 broadcast_select_fusion.1
  232.9 4.3 %convolution_bitcast_fusion = f32[768,768]{0,1:T(8,128)} fusion(bf16[1024,768]{1,0:T(8,128)(2,1)} %reshape.137, bf16[512,768]{1,0:T(8,128)(2,1)S(1)} %get-tuple-element.51, bf16[512,768]{1,0:T(8,128)(2,1)S(1)} %get-tuple-element.50), kind=kOutput, calls=%fused_computation.22 | convolution fusion | flops 1211105280 | bytes 5505024 | tf_op jit(solution)/shard_map/dot_general | solution.py:86
  237.2 3.0 %copy.22 = f32[768,768]{1,0:T(8,128)} copy(f32[768,768]{0,1:T(8,128)} %convolution_bitcast_fusion) | data formatting | bytes 4718592
  (25 shorter events, 0.4 us)
Async XLA Ops:
  7.2 1.7 copy-start
  28.0 20.1 %all-to-all-start.1 = ((bf16[16,32,896]{2,1,0:T(8,128)(2,1)}), bf16[16,32,896]{2,1,0:T(8,128)(2,1)S(1)}, u32[]{:S(2)}, u32[]{:S(2)}) async-start(bf16[16,32,896]{2,1,0:T(8,128)(2,1)} %broadcast_in_dim.95), calls=%async_computation.1 | async-start | bytes 1835008 | tf_op jit(solution)/shard_map/all_to_all | solution.py:12
  81.3 32.2 %copy-start.1 = (f32[4,768]{1,0:T(4,128)S(1)}, f32[4,768]{1,0:T(4,128)}, u32[]{:S(2)}) copy-start(f32[4,768]{1,0:T(4,128)} %param.4) | copy-start | bytes 36868
  109.9 11.2 %all-to-all-start.5 = ((f32[8,5,512]{2,1,0:T(8,128)}), f32[8,5,512]{2,1,0:T(8,128)S(1)}, u32[]{:S(2)}, u32[]{:S(2)}) async-start(f32[8,5,512]{2,1,0:T(8,128)} %broadcast_in_dim.100), calls=%async_computation.5 | async-start | bytes 262144 | tf_op jit(solution)/shard_map/all_to_all | solution.py:12
  113.2 111.3 %all-gather.3.cloned.1.call-start = ((), (), s32[]{:S(2)}) async-start(), calls=%async_computation.9 | async-start | bytes 1579008 | tf_op jit(solution)/shard_map/all_gather | solution.py:34
  181.6 50.1 %collective-permute-start = (bf16[512,768]{1,0:T(8,128)(2,1)S(1)}, bf16[512,768]{1,0:T(8,128)(2,1)}, u32[]{:S(2)}, u32[]{:S(2)}) collective-permute-start(bf16[512,768]{1,0:T(8,128)(2,1)S(1)} %bitcast.42), channel_id=1, source_target_pairs={{0,1},{1,0},{2,3},{3,2},{4,5},{5,4},{6,7},{7,6},{8,9},{9,8},{10,11... | collective-permute-start | bytes 2359304 | tf_op jit(solution)/shard_map/ppermute | solution.py:81
Sparse Core Ops, SparseCore 0:
  117.8 106.7 all-gather.2
where the time goes:
time: 248 us; the launch traced here: 247 us
  blocking collectives  87.4 us (35%)
  waiting for transfers between devices  49.3 us (20%)
  matrix products  40.5 us (16%)
  starting transfers between devices  21.2 us (9%)
  other arithmetic  20.4 us (8%)
  between operations  14.2 us (6%)
  local copies, waits for them, and re-layouts  14.1 us (6%)
    all_to_all x7, blocking collectives, exchange(): return lax.all_to_all(v, axes, 0, 0, tiled=False)  87.4 us
    all_gather x1, waiting for transfers between devices, shards(): raw_all = lax.all_gather(queries_raw.astype(bf16), ALL, axis=0, tiled=True)  28.9 us
    all_to_all x2, waiting for transfers between devices, exchange(): return lax.all_to_all(v, axes, 0, 0, tiled=False)  20.3 us
    dot_general x1, matrix products, shards(): jnp.dot(grad.astype(bf16), passages, preferred_element_type=jnp.float32)  20.3 us
    reduce_sum x1, other arithmetic, shards(): loss_part = loss_part + jnp.sum(sig, axis=1)  17 us
    dot_general x1, matrix products, shards(): lax.dot_general(all_emb, passages, (((1,), (1,)), ((), ())), preferred_el...  11.5 us
    ppermute x1, starting transfers between devices, shards(): other = lax.ppermute(mine, 'c', [(0, 1), (1, 0)])  10.9 us
    all_to_all x2, starting transfers between devices, exchange(): return lax.all_to_all(v, axes, 0, 0, tiled=False)  10.1 us
  transfers between devices with their start and end apart: 4, of which 3 were waited for; matrix products, arithmetic and copies ran while one was open for 13% of the time, Pallas kernels for 0%

commit v1 on v0

--- a/solution.py
+++ b/solution.py
@@ -31,7 +31,10 @@
     queries = nxy * plane
     scale = 1.0 / (4.0 * rows * nz * nxy)
     bf16 = jnp.bfloat16
-    raw_all = lax.all_gather(queries_raw.astype(bf16), ALL, axis=0, tiled=True)
+    raw_all = jnp.concatenate(
+        lax.all_to_all(jnp.stack([queries_raw.astype(bf16)] * lax.axis_size(ALL)), ALL, 0, 0),
+        axis=0,
+    )
     projected = jnp.dot(queries_raw, projection, precision=hp, preferred_element_type=jnp.float32)
     ids = jnp.concatenate([positives >> 14, positives >> 7 & 127, positives & 127], axis=1)
     ids = jnp.pad(ids, ((0, 0), (0, 128 - 3 * POS)))

time: 248 us -> 252 us (1.016)
  between operations: 14.2 us -> 0.86 us
  waiting for transfers between devices: 49.3 us -> 59.3 us
  starting transfers between devices: 21.2 us -> 30.1 us
  blocking collectives: 87.4 us -> 84.3 us
    all_to_all x0 -> x1, waiting for transfers between devices: none -> 35.7 us  [shards(): lax.all_to_all(jnp.stack([queries_raw.astype(bf16)] * lax.axis_size(ALL))...]
    all_gather x1 -> x0, waiting for transfers between devices: 28.9 us -> none  [shards(): raw_all = lax.all_gather(queries_raw.astype(bf16), ALL, axis=0, tiled=True)]
    all_to_all x0 -> x1, starting transfers between devices: none -> 17.1 us  [shards(): lax.all_to_all(jnp.stack([queries_raw.astype(bf16)] * lax.axis_size(ALL))...]
    ppermute x1, starting transfers between devices: 10.9 us -> 2.66 us  [shards(): other = lax.ppermute(mine, 'c', [(0, 1), (1, 0)])]
    transpose x0 -> x1, local copies, waits for them, and re-layouts: none -> 3.38 us  [shards(): raw_all.reshape(*sizes, own, dim).transpose(3, 0, 2, 1, 4, 5)]
    reshape x2 -> x1, local copies, waits for them, and re-layouts: 7.1 us -> 3.73 us  [shards(): raw_all.reshape(*sizes, own, dim).transpose(3, 0, 2, 1, 4, 5)]
    all_to_all x2, waiting for transfers between devices: 20.3 us -> 23.6 us  [exchange(): return lax.all_to_all(v, axes, 0, 0, tiled=False)]
    all_to_all x7, blocking collectives: 87.4 us -> 84.3 us  [exchange(): return lax.all_to_all(v, axes, 0, 0, tiled=False)]
  transfers between devices with their start and end apart: 4 -> 4, of which waited for: 3 -> 3; matrix products, arithmetic and copies ran while one was open for 13% -> 4% of each run, Pallas kernels for 0% -> 0%
where the time goes in v1:
time: 252 us; the launch traced here: 251 us
  blocking collectives  84.3 us (33%)
  waiting for transfers between devices  59.3 us (24%)
  matrix products  40.6 us (16%)
  starting transfers between devices  30.1 us (12%)
  other arithmetic  19.8 us (8%)
  local copies, waits for them, and re-layouts  15.8 us (6%)
    all_to_all x7, blocking collectives, exchange(): return lax.all_to_all(v, axes, 0, 0, tiled=False)  84.3 us
    all_to_all x1, waiting for transfers between devices, shards(): lax.all_to_all(jnp.stack([queries_raw.astype(bf16)] * lax.axis_size(ALL))...  35.7 us
    all_to_all x2, waiting for transfers between devices, exchange(): return lax.all_to_all(v, axes, 0, 0, tiled=False)  23.6 us
    dot_general x1, matrix products, shards(): jnp.dot(grad.astype(bf16), passages, preferred_element_type=jnp.float32)  20.3 us
    all_to_all x1, starting transfers between devices, shards(): lax.all_to_all(jnp.stack([queries_raw.astype(bf16)] * lax.axis_size(ALL))...  17.1 us
    reduce_sum x1, other arithmetic, shards(): loss_part = loss_part + jnp.sum(sig, axis=1)  17.1 us
    dot_general x1, matrix products, shards(): lax.dot_general(all_emb, passages, (((1,), (1,)), ((), ())), preferred_el...  11.5 us
    all_to_all x2, starting transfers between devices, exchange(): return lax.all_to_all(v, axes, 0, 0, tiled=False)  10.4 us
  transfers between devices with their start and end apart: 4, of which 3 were waited for; matrix products, arithmetic and copies ran while one was open for 4% of the time, Pallas kernels for 0%

profile of v1, /device:TPU:1, one launch (start us, length us, event | category | flops | bytes accessed | tf_op | source)
XLA Modules:
  0.0 250.9 jit_solution(1856981258674896422)
XLA Ops:
  0.6 0.0 copy-start
  0.6 0.8 shift-right-arithmetic_convert_fusion
  1.5 0.8 copy-done
  2.3 1.9 convolution_convert_fusion
  4.2 0.1 fusion.19
  4.4 16.1 %all_to_all.50 = bf16[8,4,896]{2,1,0:T(4,128)(2,1)S(1)} all-to-all(bf16[8,4,896]{2,1,0:T(4,128)(2,1)S(1)} %broadcast_in_dim.93), channel_id=1, replica_groups=mesh['x'=4,'z'=8,'y'=4,'c'=2] {'z'}, dimensions={0} | all-to-all | bytes 114688 | tf_op jit(solution)/shard_map/all_to_all | solution.py:12
  20.4 1.0 broadcast_in_dim.95
  21.4 6.8 %all-to-all-start.1 = ((bf16[16,32,896]{2,1,0:T(8,128)(2,1)}), bf16[16,32,896]{2,1,0:T(8,128)(2,1)S(1)}, u32[]{:S(2)}, u32[]{:S(2)}) async-start(bf16[16,32,896]{2,1,0:T(8,128)(2,1)} %broadcast_in_dim.95), calls=%async_computation.1 | async-start | bytes 1835008 | tf_op jit(solution)/shard_map/all_to_all | solution.py:12
  28.2 13.4 %all-to-all-done.1 = bf16[16,32,896]{2,1,0:T(8,128)(2,1)S(1)} async-done(((bf16[16,32,896]{2,1,0:T(8,128)(2,1)}), bf16[16,32,896]{2,1,0:T(8,128)(2,1)S(1)}, u32[]{:S(2)}, u32[]{:S(2)}) %all-to-all-start.1) | async-done | bytes 917536 | tf_op jit(solution)/shard_map/all_to_all | solution.py:12
  41.6 0.2 fusion.11
  41.8 0.6 slice_reduce_fusion.3
  42.4 11.5 %select_reduce_fusion.3 = (f32[512]{0:T(512)S(1)}, f32[512]{0:T(512)S(1)}, f32[512]{0:T(512)S(1)}, f32[512]{0:T(512)S(1)}, f32[512,4096]{1,0:T(8,128)}) fusion(s32[512]{0:T(512)S(1)} %get-tuple-element.30, s32[512]{0:T(512)S(1)} %get-tuple-element.31, s32[512]{0:T(512)S(1)} %get-tuple-element.32, s32[512]{0:T(512)S(1)} %get-tuple-element.33, ...), kind=kOutput, calls=%fused_computation.15 | convolution fusion | flops 3246389248 | bytes 15482880 | tf_op jit(solution)/shard_map/dot_general | solution.py:51
  53.9 11.2 %all_to_all.51 = f32[16,4,512]{2,1,0:T(4,128)S(1)} all-to-all(f32[16,4,512]{2,1,0:T(4,128)S(1)} %broadcast_in_dim.97), channel_id=1, replica_groups=mesh['x'=4,'z'=8,'y'=4,'c'=2] {'x','y'}, dimensions={0} | all-to-all | bytes 262144 | tf_op jit(solution)/shard_map/all_to_all | solution.py:12
  65.1 9.6 %all_to_all.52 = f32[8,4,512]{2,1,0:T(4,128)S(1)} all-to-all(f32[8,4,512]{2,1,0:T(4,128)S(1)} %broadcast_in_dim.98), channel_id=1, replica_groups=mesh['x'=4,'z'=8,'y'=4,'c'=2] {'z'}, dimensions={0} | all-to-all | bytes 131072 | tf_op jit(solution)/shard_map/all_to_all | solution.py:12
  74.8 17.1 %fusion.28 = (f32[512]{0:T(512)S(1)}, f32[512]{0:T(512)S(1)}, f32[512,4096]{1,0:T(8,128)}, f32[512]{0:T(512)S(1)}, f32[512]{0:T(512)S(1)}, /*index=5*/f32[512,40...) fusion(f32[512,4096]{1,0:T(8,128)} %get-tuple-element.60, ...), kind=kLoop, calls=%fused_computation.68 | loop fusion | flops 67104768 | bytes 41967616 | tf_op jit(solution)/shard_map/reduce_sum | solution.py:65
  92.0 10.7 %all_to_all.53 = f32[16,5,512]{2,1,0:T(8,128)S(1)} all-to-all(f32[16,5,512]{2,1,0:T(8,128)S(1)} %broadcast_in_dim.99), channel_id=1, replica_groups=mesh['x'=4,'z'=8,'y'=4,'c'=2] {'x','y'}, dimensions={0} | all-to-all | bytes 327680 | tf_op jit(solution)/shard_map/all_to_all | solution.py:12
  102.7 10.3 %all_to_all.54 = f32[8,5,512]{2,1,0:T(8,128)S(1)} all-to-all(f32[8,5,512]{2,1,0:T(8,128)S(1)} %broadcast_in_dim.100), channel_id=1, replica_groups=mesh['x'=4,'z'=8,'y'=4,'c'=2] {'z'}, dimensions={0} | all-to-all | bytes 163840 | tf_op jit(solution)/shard_map/all_to_all | solution.py:12
  113.1 0.0 copy-start.1
  113.1 20.3 %fusion.8 = bf16[512,768]{1,0:T(8,128)(2,1)S(1)} fusion(bf16[4096,768]{1,0:T(8,128)(2,1)} %param.6, f32[512,4096]{1,0:T(8,128)} %get-tuple-element.40, f32[512,4096]{1,0:T(8,128)} %get-tuple-element.46, f32[512,4096]{1,0:T(8,128)} %get-tuple-element.43, f32[512,4096]{1,0:T(8,128)} %get-tuple-element.34, f32[512]{0:T(512)S(1)} %bitcast.53, ...), kind=kOutput, calls=%fused_computation.26 | convolution fusion | flops 3274047488 | bytes 40648704 | tf_op jit(solution)/shard_map/dot_general | solution.py:74
  133.4 13.4 %all_to_all.55 = bf16[16,32,768]{2,1,0:T(8,128)(2,1)S(1)} all-to-all(bf16[16,32,768]{2,1,0:T(8,128)(2,1)S(1)} %bitcast.41), channel_id=1, replica_groups=mesh['x'=4,'z'=8,'y'=4,'c'=2] {'x','y'}, dimensions={0} | all-to-all | bytes 1572864 | tf_op jit(solution)/shard_map/all_to_all | solution.py:12
  146.8 0.1 reduce_sum.181
  146.9 13.1 %all_to_all.56 = bf16[8,32,768]{2,1,0:T(8,128)(2,1)S(1)} all-to-all(bf16[8,32,768]{2,1,0:T(8,128)(2,1)S(1)} %broadcast_in_dim.109), channel_id=1, replica_groups=mesh['x'=4,'z'=8,'y'=4,'c'=2] {'z'}, dimensions={0} | all-to-all | bytes 786432 | tf_op jit(solution)/shard_map/all_to_all | solution.py:12
  160.0 0.1 convert_reduce_fusion
  160.1 1.0 broadcast_in_dim.110
  161.1 3.6 %all-to-all-start.8 = ((bf16[16,32,768]{2,1,0:T(8,128)(2,1)}), bf16[16,32,768]{2,1,0:T(8,128)(2,1)S(1)}, u32[]{:S(2)}, u32[]{:S(2)}) async-start(bf16[16,32,768]{2,1,0:T(8,128)(2,1)} %broadcast_in_dim.110), calls=%async_computation.8 | async-start | bytes 1572864 | tf_op jit(solution)/shard_map/all_to_all | solution.py:12
  164.7 0.0 copy-done.1
  164.7 10.3 %all-to-all-done.8 = bf16[16,32,768]{2,1,0:T(8,128)(2,1)S(1)} async-done(((bf16[16,32,768]{2,1,0:T(8,128)(2,1)}), bf16[16,32,768]{2,1,0:T(8,128)(2,1)S(1)}, u32[]{:S(2)}, u32[]{:S(2)}) %all-to-all-start.8) | async-done | bytes 786464 | tf_op jit(solution)/shard_map/all_to_all | solution.py:12
  175.0 1.5 stack.20
  176.6 17.1 %all-to-all-start.9 = ((bf16[256,4,768]{2,1,0:T(4,128)(2,1)}), bf16[256,4,768]{2,1,0:T(4,128)(2,1)}, u32[]{:S(2)}, u32[]{:S(2)}) async-start(bf16[256,4,768]{2,1,0:T(4,128)(2,1)} %stack.20), calls=%async_computation.9 | async-start | bytes 3145728 | tf_op jit(solution)/shard_map/all_to_all | solution.py:35
  193.7 2.7 %collective-permute-start = (bf16[512,768]{1,0:T(8,128)(2,1)S(1)}, bf16[512,768]{1,0:T(8,128)(2,1)}, u32[]{:S(2)}, u32[]{:S(2)}) collective-permute-start(bf16[512,768]{1,0:T(8,128)(2,1)S(1)} %bitcast.38), channel_id=1, source_target_pairs={{0,1},{1,0},{2,3},{3,2},{4,5},{5,4},{6,7},{7,6},{8,9},{9,8},{10,11... | collective-permute-start | bytes 2359304 | tf_op jit(solution)/shard_map/ppermute | solution.py:84
  196.3 0.6 dynamic-slice_bitcast_fusion
  196.9 2.6 %fusion.13 = f32[4,768]{1,0:T(4,128)} fusion(f32[768,768]{1,0:T(8,128)S(1)} %copy-done, f32[32,768]{1,0:T(8,128)S(1)} %convert_reduce_fusion, s32[]{:T(128)S(6)} %select_n.53), kind=kOutput, calls=%fused_computation.43 | convolution fusion | flops 28311552 | bytes 2383876 | tf_op jit(solution)/shard_map/dot_general | solution.py:80
  199.5 35.7 %all-to-all-done.9 = bf16[256,4,768]{2,1,0:T(4,128)(2,1)} async-done(((bf16[256,4,768]{2,1,0:T(4,128)(2,1)}), bf16[256,4,768]{2,1,0:T(4,128)(2,1)}, u32[]{:S(2)}, u32[]{:S(2)}) %all-to-all-start.9) | async-done | bytes 1572896 | tf_op jit(solution)/shard_map/all_to_all | solution.py:35
  235.2 3.4 %copy.18 = bf16[2,4,4,8,4,768]{5,4,3,2,1,0:T(4,128)(2,1)} copy(bf16[2,4,4,8,4,768]{5,4,0,2,3,1:T(4,128)(2,1)} %bitcast.24) | data formatting | bytes 3145728 | tf_op jit(solution)/shard_map/transpose | solution.py:88
  238.6 3.7 %reshape.135 = bf16[1024,768]{1,0:T(8,128)(2,1)} reshape(bf16[2,4,4,8,4,768]{5,4,3,2,1,0:T(4,128)(2,1)} %copy.18) | data formatting | bytes 3145728 | tf_op jit(solution)/shard_map/reshape | solution.py:88
  242.3 0.0 collective-permute-done
  242.3 1.2 broadcast_select_fusion.1
  243.5 4.3 %convolution_bitcast_fusion = f32[768,768]{0,1:T(8,128)} fusion(bf16[1024,768]{1,0:T(8,128)(2,1)} %reshape.135, bf16[512,768]{1,0:T(8,128)(2,1)S(1)} %get-tuple-element.48, bf16[512,768]{1,0:T(8,128)(2,1)S(1)} %get-tuple-element.47), kind=kOutput, calls=%fused_computation.22 | convolution fusion | flops 1211105280 | bytes 5505024 | tf_op jit(solution)/shard_map/dot_general | solution.py:89
  247.8 3.0 %copy.19 = f32[768,768]{1,0:T(8,128)} copy(f32[768,768]{0,1:T(8,128)} %convolution_bitcast_fusion) | data formatting | bytes 4718592
  (27 shorter events, 0.4 us)
Async XLA Ops:
  0.6 1.7 copy-start
  21.4 20.1 %all-to-all-start.1 = ((bf16[16,32,896]{2,1,0:T(8,128)(2,1)}), bf16[16,32,896]{2,1,0:T(8,128)(2,1)S(1)}, u32[]{:S(2)}, u32[]{:S(2)}) async-start(bf16[16,32,896]{2,1,0:T(8,128)(2,1)} %broadcast_in_dim.95), calls=%async_computation.1 | async-start | bytes 1835008 | tf_op jit(solution)/shard_map/all_to_all | solution.py:12
  113.1 51.6 %copy-start.1 = (f32[4,768]{1,0:T(4,128)S(1)}, f32[4,768]{1,0:T(4,128)}, u32[]{:S(2)}) copy-start(f32[4,768]{1,0:T(4,128)} %param.4) | copy-start | bytes 36868
  161.1 13.9 %all-to-all-start.8 = ((bf16[16,32,768]{2,1,0:T(8,128)(2,1)}), bf16[16,32,768]{2,1,0:T(8,128)(2,1)S(1)}, u32[]{:S(2)}, u32[]{:S(2)}) async-start(bf16[16,32,768]{2,1,0:T(8,128)(2,1)} %broadcast_in_dim.110), calls=%async_computation.8 | async-start | bytes 1572864 | tf_op jit(solution)/shard_map/all_to_all | solution.py:12
  176.6 58.6 %all-to-all-start.9 = ((bf16[256,4,768]{2,1,0:T(4,128)(2,1)}), bf16[256,4,768]{2,1,0:T(4,128)(2,1)}, u32[]{:S(2)}, u32[]{:S(2)}) async-start(bf16[256,4,768]{2,1,0:T(4,128)(2,1)} %stack.20), calls=%async_computation.9 | async-start | bytes 3145728 | tf_op jit(solution)/shard_map/all_to_all | solution.py:35
  193.7 48.6 %collective-permute-start = (bf16[512,768]{1,0:T(8,128)(2,1)S(1)}, bf16[512,768]{1,0:T(8,128)(2,1)}, u32[]{:S(2)}, u32[]{:S(2)}) collective-permute-start(bf16[512,768]{1,0:T(8,128)(2,1)S(1)} %bitcast.38), channel_id=1, source_target_pairs={{0,1},{1,0},{2,3},{3,2},{4,5},{5,4},{6,7},{7,6},{8,9},{9,8},{10,11... | collective-permute-start | bytes 2359304 | tf_op jit(solution)/shard_map/ppermute | solution.py:84
